TPU v7x, 32 devices: a whole 2x2x4 slice. The times are simulated.
32 devices in a mesh: row: 4 (over y, core), col: 8 (over z, x).
Axes of the slice: x: 2, y: 2, z: 4, core: 2. Of those that a mesh axis runs over, the one named last changes fastest.
Arguments:
- left: bfloat16 [8, 16, 512, 256], P('row', 'col'), may hold values from -0.11767578 to 0.11767578
- right: bfloat16 [8, 16, 512, 256], P('row', 'col'), may hold values from -6 to 6
- lower_inverse: bfloat16 [2, 512, 512], P(None, 'row'), as said below
- upper_inverse: bfloat16 [2, 512, 512], P(None, None, 'col'), as said below
- ranks: int32 [8, 16], P('row', 'col'), may hold values from 16 to 256, as said below
Outputs:
- right_out: bfloat16 [8, 16, 512, 256], P('row', 'col')
Inputs may be any that keep to these rules, and one draw needn't show every extreme that they name: Tile ranks: every row of `ranks` contains at least one entry equal to 256; all entries lie in 4..256. Each lower_inverse[k] is lower triangular with a positive diagonal. Each upper_inverse[k] is upper triangular with a positive diagonal.
All inputs are finite; a program needn't handle non-finite values.
Results may differ from a plain program's by a relative error of at most 0.009.
Values may be sent and summed in bfloat16 or wider, within the bound.
A program may use at most 64 MiB of HBM per device.

v0:
```python
import jax
import jax.numpy as jnp
from jax import lax
from jax.sharding import PartitionSpec as P


def broadcast(value, axis, source):
    kept = jnp.where(lax.axis_index(axis) == source, value, 0).astype(value.dtype)
    return lax.psum(kept, axis)


def update_tiles(
    left, right, col_left, col_right, row_left, row_right, tile_rows, tile_cols, panel
):
    core = jnp.einsum("abr,cbs->acrs", col_right, row_left, preferred_element_type=jnp.float32)
    intersection = jnp.einsum("acbr,abs->acrs", left, col_left, preferred_element_type=jnp.float32)
    mixed = jnp.einsum(
        "acrs,acst->acrt", intersection, core, precision=lax.Precision.HIGHEST
    ).astype(jnp.bfloat16)
    change = jnp.einsum("cbt,acrt->acbr", row_right, mixed, preferred_element_type=jnp.float32)
    fresh = (right.astype(jnp.float32) - change).astype(jnp.bfloat16)
    below = (tile_rows > panel)[:, None, None, None]
    trail = below & (tile_cols > panel)[None, :, None, None]
    on_panel = below & (tile_cols == panel)[None, :, None, None]
    kept = jnp.where(on_panel, col_right[:, None], right)
    return jnp.where(trail, fresh, kept)


def body(left, right, lower_inverse, upper_inverse, ranks):
    slots = lax.broadcasted_iota(jnp.int32, ranks.shape + (left.shape[3],), 2)
    keep = (slots < ranks[:, :, None]).astype(jnp.bfloat16)
    left = left * keep[:, :, None, :]
    right = right * keep[:, :, None, :]
    row_count = lax.axis_size("row")
    col_count = lax.axis_size("col")
    row_index = lax.axis_index("row")
    col_index = lax.axis_index("col")
    tile_rows = jnp.arange(left.shape[0], dtype=jnp.int32) * row_count + row_index
    tile_cols = jnp.arange(left.shape[1], dtype=jnp.int32) * col_count + col_index
    full_lower = lax.all_gather(lower_inverse, "row", axis=1, tiled=True)
    full_upper = lax.all_gather(upper_inverse, "col", axis=2, tiled=True)
    for panel in range(lower_inverse.shape[0]):

        def solve_column(factor):
            return jnp.einsum(
                "bc,abr->acr", full_upper[panel], factor, preferred_element_type=jnp.float32
            ).astype(jnp.bfloat16)

        def solve_row(factor):
            return jnp.einsum(
                "cb,jbr->jcr", full_lower[panel], factor, preferred_element_type=jnp.float32
            ).astype(jnp.bfloat16)

        solved_col = lax.cond(col_index == panel, solve_column, lambda factor: factor, right[:, 0])
        col_left, col_right = (
            broadcast(left[:, 0], "col", panel),
            broadcast(solved_col, "col", panel),
        )
        solved_row = lax.cond(row_index == panel, solve_row, lambda factor: factor, left[0])
        row_left, row_right = (
            broadcast(solved_row, "row", panel),
            broadcast(right[0], "row", panel),
        )
        right = update_tiles(
            left, right, col_left, col_right, row_left, row_right, tile_rows, tile_cols, panel
        )
    return right


def solution(mesh):
    placed = (
        P("row", "col", None, None),
        P("row", "col", None, None),
        P(None, "row", None),
        P(None, None, "col"),
        P("row", "col"),
    )
    return jax.shard_map(
        body, mesh=mesh, in_specs=placed, out_specs=P("row", "col", None, None), check_vma=False
    )
```

profile of v0, /device:TPU:0, one launch (start us, length us, event | category | flops | bytes accessed | tf_op | source)
XLA Modules:
  0.0 327.3 jit_solution(1950935950600516134)
XLA Ops:
  6.5 1.7 copy.21
  8.2 0.0 all-gather.5.cloned.1.call-update
  8.3 0.0 all-gather.3.cloned.1.call-start
  8.3 0.7 all-gather.3.cloned.1.call-update
  9.0 0.0 all-reduce.11.cloned.1.call-start
  9.1 0.8 compare_convert_fusion
  9.8 1.7 broadcast_multiply_fusion
  11.5 0.0 copy-start.1
  11.5 1.2 select_bitcast_fusion
  12.7 39.6 %all-gather.5.cloned.1.call-done = bf16[2,512,512]{1,0,2:T(2,128)(2,1)} async-done(((bf16[2,512,64]{1,0,2:T(2,128)(2,1)}), bf16[2,512,512]{1,0,2:T(2,128)(2,1)}) %all-gather.5.cloned.1.call-update) | async-done | bytes 1048592 | tf_op jit(solution)/shard_map/all_gather | solution.py:41
  52.4 5.2 %conditional.5 = (bf16[2,512,256]{1,2,0:T(8,128)(2,1)S(1)}) conditional(s32[]{:T(128)} %convert_element_type.73, (bf16[2,512,256]{2,1,0:T(8,128)(2,1)S(1)}) %tuple.40, (bf16[2,512,512]{1,0,2:T(2,128)(2,1)}, bf16[2,512,256]{2,1,0:T(8,128)(2,1)S(1)}) %tuple.30), branch_computations={%region_4.5_spmd, %region_5.6_spmd} | conditional | flops 268697600 | bytes 3670024 | solution.py:54
  52.4 3.7 %copy.23 = bf16[2,512,512]{2,1,0:T(8,128)(2,1)} copy(bf16[2,512,512]{1,0,2:T(2,128)(2,1)} %get-tuple-element.55) | data formatting | bytes 2097152 | tf_op jit(solution)/shard_map
  56.0 1.5 fusion.3
  57.5 0.9 broadcast_select_fusion.2
  58.4 0.0 all-reduce.11.cloned.1.call-update
  58.4 0.0 all-reduce.15.cloned.1.call-start
  58.5 0.2 copy.19
  58.8 0.9 fusion.17
  59.6 9.8 %all-gather.3.cloned.1.call-done = bf16[2,512,512]{2,1,0:T(8,128)(2,1)} async-done(((bf16[2,128,512]{2,1,0:T(8,128)(2,1)}), bf16[2,512,512]{2,1,0:T(8,128)(2,1)}) %all-gather.3.cloned.1.call-update) | async-done | bytes 1048592 | tf_op jit(solution)/shard_map/all_gather | solution.py:40
  69.4 1.5 conditional.4
  69.4 1.5 fusion
  71.0 0.8 broadcast_select_fusion.3
  71.8 0.0 all-reduce.15.cloned.1.call-update
  71.8 0.0 all-reduce.9.cloned.1.call-start
  71.9 0.1 broadcast_and_fusion.2
  72.0 79.4 %all-reduce.11.cloned.1.call-done = (bf16[2,512,256]{1,2,0:T(8,128)(2,1)}, bf16[2,512,256]{2,1,0:T(8,128)(2,1)}) async-done(((bf16[2,512,256]{1,2,0:T(8,128)(2,1)}, bf16[2,512,256]{2,1,0:T(8,128)(2,1)}), (bf16[2,512,256]{1,2,0:T(8,128)(2,1)}, bf16[2,512,256]{2,1,0:T(8,128)(2,1)})) %all-reduce.11.cloned.1.call-update) | async-done | bytes 1048592 | tf_op jit(solution)/shard_map/psum | solution.py:9
  151.4 2.1 copy.26
  153.5 1.6 fusion.24
  155.1 34.3 %all-reduce.15.cloned.1.call-done = (bf16[2,512,256]{2,1,0:T(8,128)(2,1)}, bf16[2,512,256]{1,2,0:T(8,128)(2,1)}) async-done(((bf16[2,512,256]{2,1,0:T(8,128)(2,1)}, bf16[2,512,256]{1,2,0:T(8,128)(2,1)}), (bf16[2,512,256]{2,1,0:T(8,128)(2,1)}, bf16[2,512,256]{1,2,0:T(8,128)(2,1)})) %all-reduce.15.cloned.1.call-update) | async-done | bytes 1048592 | tf_op jit(solution)/shard_map/psum | solution.py:9
  189.4 1.7 fusion.22
  191.1 0.8 copy.69
  191.9 0.0 copy-start.2
  191.9 0.0 copy-start.9
  191.9 1.2 convolution_convert_fusion.5
  193.1 0.0 copy-done.2
  193.1 0.1 copy-done.9
  193.2 0.2 copy-done.10
  193.4 0.6 fusion.10
  194.0 0.0 copy-start.4
  194.0 0.8 slice_bitcast_fusion.4
  194.9 0.9 copy-done
  195.8 1.3 conditional.7
  195.8 1.3 copy.53
  197.1 0.8 broadcast_select_fusion
  197.9 0.0 all-reduce.9.cloned.1.call-update
  198.0 0.0 all-reduce.13.cloned.1.call-start
  198.0 0.0 copy-start.5
  198.1 0.8 broadcast_select_fusion.1
  198.9 0.5 copy-done.5
  199.4 0.9 fusion.16
  200.3 0.0 all-reduce.13.cloned.1.call-update
  200.3 0.1 broadcast_and_fusion.3
  200.4 76.7 %all-reduce.9.cloned.1.call-done = (bf16[2,512,256]{1,2,0:T(8,128)(2,1)}, bf16[2,512,256]{2,1,0:T(8,128)(2,1)}) async-done(((bf16[2,512,256]{1,2,0:T(8,128)(2,1)}, bf16[2,512,256]{2,1,0:T(8,128)(2,1)}), (bf16[2,512,256]{1,2,0:T(8,128)(2,1)}, bf16[2,512,256]{2,1,0:T(8,128)(2,1)})) %all-reduce.9.cloned.1.call-update) | async-done | bytes 1048592 | tf_op jit(solution)/shard_map/psum | solution.py:9
  277.1 2.1 copy.33
  279.2 0.5 fusion.20
  279.7 35.3 %all-reduce.13.cloned.1.call-done = (bf16[2,512,256]{2,1,0:T(8,128)(2,1)}, bf16[2,512,256]{1,2,0:T(8,128)(2,1)}) async-done(((bf16[2,512,256]{2,1,0:T(8,128)(2,1)}, bf16[2,512,256]{1,2,0:T(8,128)(2,1)}), (bf16[2,512,256]{2,1,0:T(8,128)(2,1)}, bf16[2,512,256]{1,2,0:T(8,128)(2,1)})) %all-reduce.13.cloned.1.call-update) | async-done | bytes 1048592 | tf_op jit(solution)/shard_map/psum | solution.py:9
  315.1 1.5 fusion.18
  316.6 0.8 copy.68
  317.4 0.0 copy-start.6
  317.4 1.2 convolution_convert_fusion.4
  318.6 0.0 copy-done.6
  318.6 0.1 copy-done.8
  318.8 0.2 copy-done.11
  318.9 1.6 fusion.11
  (17 shorter events, 0.1 us)
Async XLA Ops:
  6.5 45.8 %all-gather.5.cloned.1.call-start = ((), (), s32[]{:S(2)}) async-start(), calls=%async_computation.1 | async-start | bytes 1179648 | tf_op jit(solution)/shard_map/all_gather | solution.py:41
  8.3 61.2 %all-gather.3.cloned.1.call-start = ((), (), s32[]{:S(2)}) async-start(), calls=%async_computation | async-start | bytes 1310720 | tf_op jit(solution)/shard_map/all_gather | solution.py:40
  9.0 142.4 %all-reduce.11.cloned.1.call-start = ((), (), s32[]{:S(2)}) async-start(), calls=%async_computation.3 | async-start | bytes 2097152 | tf_op jit(solution)/shard_map/psum | solution.py:9
  11.5 47.2 %copy-start.1 = (bf16[2,2,512,256]{3,2,1,0:T(8,128)(2,1)}, bf16[2,2,512,256]{3,2,1,0:T(8,128)(2,1)S(1)}, u32[]{:S(2)}) copy-start(bf16[2,2,512,256]{3,2,1,0:T(8,128)(2,1)S(1)} %get-tuple-element.76) | copy-start | bytes 3145732
  58.4 131.0 %all-reduce.15.cloned.1.call-start = ((), (), s32[]{:S(2)}) async-start(), calls=%async_computation.5 | async-start | bytes 2097152 | tf_op jit(solution)/shard_map/psum | solution.py:9
  71.8 205.2 %all-reduce.9.cloned.1.call-start = ((), (), s32[]{:S(2)}) async-start(), calls=%async_computation.2 | async-start | bytes 2097152 | tf_op jit(solution)/shard_map/psum | solution.py:9
  191.9 1.2 copy-start.2
  191.9 1.3 copy-start.9
  191.9 1.5 copy-start.10
  194.0 1.8 copy-start.4
  194.0 1.8 copy-start
  198.0 117.1 %all-reduce.13.cloned.1.call-start = ((), (), s32[]{:S(2)}) async-start(), calls=%async_computation.4 | async-start | bytes 2097152 | tf_op jit(solution)/shard_map/psum | solution.py:9
  198.0 1.4 copy-start.5
  277.1 2.1 copy-start.7
  279.2 35.9 %copy-start.3 = (bf16[2,512,256]{1,2,0:T(8,128)(2,1)S(1)}, bf16[2,512,256]{1,2,0:T(8,128)(2,1)}, u32[]{:S(2)}) copy-start(bf16[2,512,256]{1,2,0:T(8,128)(2,1)} %get-tuple-element.65) | copy-start | bytes 1572868
  317.4 1.2 copy-start.6
  317.4 1.3 copy-start.8
  317.4 1.5 copy-start.11
Sparse Core Ops, SparseCore 0:
  9.5 42.8 all-gather.4
  53.9 15.4 all-gather.2
  73.0 78.3 all-reduce.10
  153.9 35.4 all-reduce.14
  198.1 78.9 all-reduce.8
  279.5 35.4 all-reduce.12
where the time goes:
time: 328 us; the launch traced here: 327 us
  waiting for transfers between devices  276 us (84%)
  local copies, waits for them, and re-layouts  15.6 us (5%)
  between operations  13.7 us (4%)
  matrix products  12.8 us (4%)
  other arithmetic  8.93 us (3%)
    psum x4, waiting for transfers between devices, broadcast(): return lax.psum(kept, axis)  226 us
    all_gather x1, waiting for transfers between devices, body(): full_upper = lax.all_gather(upper_inverse, 'col', axis=2, tiled=True)  39.6 us
    all_gather x1, waiting for transfers between devices, body(): full_lower = lax.all_gather(lower_inverse, 'row', axis=1, tiled=True)  9.83 us
  transfers between devices with their start and end apart: 6, of which 6 were waited for; matrix products, arithmetic and copies ran while one was open for 6% of the time, Pallas kernels for 0%

commit v1 on v0

--- a/solution.py
+++ b/solution.py
@@ -1,7 +1,27 @@
+import functools
 import jax
 import jax.numpy as jnp
 from jax import lax
 from jax.sharding import PartitionSpec as P
+
+
+def close_counts(local_values, ax_name):
+    n_slots = lax.axis_size(ax_name)
+    log = tuple(((dev, (dev + 1) % n_slots) for dev in range(n_slots)))
+    rack = tuple(((dev, (dev - 1) % n_slots) for dev in range(n_slots)))
+    o_now, local_next = ([local_values], [local_values])
+    for _ in range(n_slots // 2):
+        outer = lax.ppermute(o_now[-1], axis_name=ax_name, perm=log)
+        o_now.append(outer)
+    for _ in [*range((n_slots - 1) // 2)]:
+        passed = lax.ppermute(local_next[-1], axis_name=ax_name, perm=rack)
+        local_next.append(passed)
+    even = jnp.concatenate([*o_now[::-1], *local_next[1:]], axis=1)
+    v_now = lax.axis_index(ax_name)
+    return jnp.roll(even, (v_now - n_slots // 2) * local_values.shape[1], axis=1)
+
+
+put_files_over_axis = functools.partial(close_counts, ax_name="row")
 
 
 def broadcast(value, axis, source):
@@ -37,7 +57,7 @@
     col_index = lax.axis_index("col")
     tile_rows = jnp.arange(left.shape[0], dtype=jnp.int32) * row_count + row_index
     tile_cols = jnp.arange(left.shape[1], dtype=jnp.int32) * col_count + col_index
-    full_lower = lax.all_gather(lower_inverse, "row", axis=1, tiled=True)
+    full_lower = put_files_over_axis(lower_inverse)
     full_upper = lax.all_gather(upper_inverse, "col", axis=2, tiled=True)
     for panel in range(lower_inverse.shape[0]):
 

time: 328 us -> 310 us (0.945)
  waiting for transfers between devices: 276 us -> 242 us
  local copies, waits for them, and re-layouts: 15.6 us -> 27 us
  starting transfers between devices: 0.21 us -> 5.2 us
    psum x4, waiting for transfers between devices: 226 us -> 213 us  [broadcast(): return lax.psum(kept, axis)]
    all_gather x1, waiting for transfers between devices: 39.6 us -> 27.7 us  [body(): full_upper = lax.all_gather(upper_inverse, 'col', axis=2, tiled=True)]
    all_gather x1 -> x0, waiting for transfers between devices: 9.83 us -> none  [body(): full_lower = lax.all_gather(lower_inverse, 'row', axis=1, tiled=True)]
    unnamed x25 -> x34, local copies, waits for them, and re-layouts: 3.88 us -> 11.1 us
    ppermute x0 -> x3, starting transfers between devices: none -> 5.03 us  [the longest x2 3.01 us: close_counts(): outer = lax.ppermute(o_now[-1], axis_name=ax_name, perm=log)]
  transfers between devices with their start and end apart: 6 -> 8, of which waited for: 6 -> 7; matrix products, arithmetic and copies ran while one was open for 6% -> 11% of each run, Pallas kernels for 0% -> 0%
where the time goes in v1:
time: 310 us; the launch traced here: 309 us
  waiting for transfers between devices  242 us (78%)
  local copies, waits for them, and re-layouts  27 us (9%)
  between operations  13.4 us (4%)
  matrix products  12.9 us (4%)
  other arithmetic  8.86 us (3%)
  starting transfers between devices  5.2 us (2%)
    psum x4, waiting for transfers between devices, broadcast(): return lax.psum(kept, axis)  213 us
    all_gather x1, waiting for transfers between devices, body(): full_upper = lax.all_gather(upper_inverse, 'col', axis=2, tiled=True)  27.7 us
    unnamed x34, local copies, waits for them, and re-layouts  11.1 us
    select_n x7, other arithmetic, broadcast(): jnp.where(lax.axis_index(axis) == source, value, 0).astype(value.dtype)  6.25 us
  transfers between devices with their start and end apart: 8, of which 7 were waited for; matrix products, arithmetic and copies ran while one was open for 11% of the time, Pallas kernels for 0%

profile of v1, /device:TPU:0, one launch (start us, length us, event | category | flops | bytes accessed | tf_op | source)
XLA Modules:
  0.0 309.3 jit_solution(7584305501647721036)
XLA Ops:
  6.5 1.7 copy.21
  8.2 0.0 all-gather.2.cloned.1.call-update
  8.2 0.0 all-reduce.11.cloned.1.call-start
  8.3 0.5 collective-permute-start
  8.8 2.0 collective-permute-start.2
  10.8 0.8 compare_convert_fusion
  11.6 1.7 broadcast_multiply_fusion
  13.3 1.2 select_bitcast_fusion
  14.5 0.8 collective-permute-done
  15.3 2.5 collective-permute-start.1
  17.8 0.8 slice_bitcast_fusion.6
  18.6 1.3 copy.19
  19.9 0.8 fusion.17
  20.7 0.6 collective-permute-done.1
  21.4 1.7 constant_dynamic-update-slice_fusion.7
  23.1 1.7 constant_dynamic-update-slice_fusion.6
  24.7 27.7 %all-gather.2.cloned.1.call-done = bf16[2,512,512]{1,0,2:T(2,128)(2,1)} async-done(((bf16[2,512,64]{1,0,2:T(2,128)(2,1)}), bf16[2,512,512]{1,0,2:T(2,128)(2,1)}) %all-gather.2.cloned.1.call-update) | async-done | bytes 1048592 | tf_op jit(solution)/shard_map/all_gather | solution.py:61
  52.4 5.2 %conditional.5 = (bf16[2,512,256]{1,2,0:T(8,128)(2,1)S(1)}) conditional(s32[]{:T(128)} %convert_element_type.73, (bf16[2,512,256]{2,1,0:T(8,128)(2,1)S(1)}) %tuple.40, (bf16[2,512,512]{1,0,2:T(2,128)(2,1)}, bf16[2,512,256]{2,1,0:T(8,128)(2,1)S(1)}) %tuple.30), branch_computations={%region_4.5_spmd, %region_5.6_spmd} | conditional | flops 268697600 | bytes 3670024 | solution.py:74
  52.4 3.7 %copy.23 = bf16[2,512,512]{2,1,0:T(8,128)(2,1)} copy(bf16[2,512,512]{1,0,2:T(2,128)(2,1)} %get-tuple-element.55) | data formatting | bytes 2097152 | tf_op jit(solution)/shard_map
  56.1 1.5 fusion.3
  57.6 0.8 broadcast_select_fusion.2
  58.4 0.0 all-reduce.11.cloned.1.call-update
  58.5 0.0 all-reduce.15.cloned.1.call-start
  58.5 0.1 copy-done.5
  58.6 0.7 constant_dynamic-update-slice_fusion.5
  59.3 0.7 constant_dynamic-update-slice_fusion.4
  60.0 1.7 constant_dynamic-update-slice_fusion.3
  61.8 1.7 constant_dynamic-update-slice_fusion.2
  63.5 0.8 constant_dynamic-update-slice_fusion.1
  64.2 0.7 constant_dynamic-update-slice_fusion
  65.0 2.3 constant_dynamic-slice_fusion
  67.3 1.5 conditional.4
  67.3 1.5 fusion
  68.8 0.8 broadcast_select_fusion.3
  69.6 0.0 all-reduce.15.cloned.1.call-update
  69.6 0.0 all-reduce.9.cloned.1.call-start
  69.7 0.1 broadcast_and_fusion.2
  69.8 64.5 %all-reduce.11.cloned.1.call-done = (bf16[2,512,256]{1,2,0:T(8,128)(2,1)}, bf16[2,512,256]{2,1,0:T(8,128)(2,1)}) async-done(((bf16[2,512,256]{1,2,0:T(8,128)(2,1)}, bf16[2,512,256]{2,1,0:T(8,128)(2,1)}), (bf16[2,512,256]{1,2,0:T(8,128)(2,1)}, bf16[2,512,256]{2,1,0:T(8,128)(2,1)})) %all-reduce.11.cloned.1.call-update) | async-done | bytes 1048592 | tf_op jit(solution)/shard_map/psum | solution.py:29
  134.2 2.0 copy.26
  136.3 36.1 %all-reduce.15.cloned.1.call-done = (bf16[2,512,256]{2,1,0:T(8,128)(2,1)}, bf16[2,512,256]{1,2,0:T(8,128)(2,1)}) async-done(((bf16[2,512,256]{2,1,0:T(8,128)(2,1)}, bf16[2,512,256]{1,2,0:T(8,128)(2,1)}), (bf16[2,512,256]{2,1,0:T(8,128)(2,1)}, bf16[2,512,256]{1,2,0:T(8,128)(2,1)})) %all-reduce.15.cloned.1.call-update) | async-done | bytes 1048592 | tf_op jit(solution)/shard_map/psum | solution.py:29
  172.4 1.7 fusion.22
  174.1 0.8 copy.69
  175.0 0.5 fusion.24
  175.5 1.2 convolution_convert_fusion.5
  176.7 0.6 fusion.10
  177.3 0.9 slice_bitcast_fusion.4
  178.2 0.2 copy-done.6
  178.5 1.3 conditional.7
  178.5 1.3 copy.53
  179.7 0.8 broadcast_select_fusion
  180.6 0.0 all-reduce.13.cloned.1.call-start
  180.7 0.2 conditional.6
  180.9 0.8 broadcast_select_fusion.1
  181.7 0.1 copy-done.7
  181.8 0.8 fusion.16
  182.7 0.1 broadcast_and_fusion.3
  182.7 76.9 %all-reduce.9.cloned.1.call-done = (bf16[2,512,256]{1,2,0:T(8,128)(2,1)}, bf16[2,512,256]{2,1,0:T(8,128)(2,1)}) async-done(((bf16[2,512,256]{1,2,0:T(8,128)(2,1)}, bf16[2,512,256]{2,1,0:T(8,128)(2,1)}), (bf16[2,512,256]{1,2,0:T(8,128)(2,1)}, bf16[2,512,256]{2,1,0:T(8,128)(2,1)})) %all-reduce.9.cloned.1.call-update) | async-done | bytes 1048592 | tf_op jit(solution)/shard_map/psum | solution.py:29
  259.6 1.3 copy.33
  261.0 1.6 fusion.20
  262.5 35.1 %all-reduce.13.cloned.1.call-done = (bf16[2,512,256]{2,1,0:T(8,128)(2,1)}, bf16[2,512,256]{1,2,0:T(8,128)(2,1)}) async-done(((bf16[2,512,256]{2,1,0:T(8,128)(2,1)}, bf16[2,512,256]{1,2,0:T(8,128)(2,1)}), (bf16[2,512,256]{2,1,0:T(8,128)(2,1)}, bf16[2,512,256]{1,2,0:T(8,128)(2,1)})) %all-reduce.13.cloned.1.call-update) | async-done | bytes 1048592 | tf_op jit(solution)/shard_map/psum | solution.py:29
  297.6 1.5 fusion.18
  299.1 0.8 copy.68
  300.0 1.2 convolution_convert_fusion.4
  301.1 1.6 fusion.11
  (31 shorter events, 0.1 us)
Async XLA Ops:
  6.5 45.9 %all-gather.2.cloned.1.call-start = ((), (), s32[]{:S(2)}) async-start(), calls=%async_computation | async-start | bytes 1179648 | tf_op jit(solution)/shard_map/all_gather | solution.py:61
  8.2 126.0 %all-reduce.11.cloned.1.call-start = ((), (), s32[]{:S(2)}) async-start(), calls=%async_computation.2 | async-start | bytes 2097152 | tf_op jit(solution)/shard_map/psum | solution.py:29
  8.3 7.0 %collective-permute-start = (bf16[2,128,512]{2,1,0:T(8,128)(2,1)}, bf16[2,128,512]{2,1,0:T(8,128)(2,1)}, u32[]{:S(2)}, u32[]{:S(2)}) collective-permute-start(bf16[2,128,512]{2,1,0:T(8,128)(2,1)} %param.15), channel_id=1, source_target_pairs={{0,8},{8,16},{16,24},{24,0},{1,9},{9,17},{17,25},{25,1},{2,10},{10... | collective-permute-start | bytes 786440 | tf_op jit(solution)/shard_map/ppermute | solution.py:14
  8.8 50.5 %collective-permute-start.2 = (bf16[2,128,512]{2,1,0:T(8,128)(2,1)}, bf16[2,128,512]{2,1,0:T(8,128)(2,1)S(1)}, u32[]{:S(2)}, u32[]{:S(2)}) collective-permute-start(bf16[2,128,512]{2,1,0:T(8,128)(2,1)} %param.15), channel_id=1, source_target_pairs={{0,24},{8,0},{16,8},{24,16},{1,25},{9,1},{17,9},{25,17},{2,26},{10... | collective-permute-start | bytes 786440 | tf_op jit(solution)/shard_map/ppermute | solution.py:17
  13.2 6.6 %copy-start.1 = (bf16[2,2,512,256]{3,2,1,0:T(8,128)(2,1)}, bf16[2,2,512,256]{3,2,1,0:T(8,128)(2,1)S(1)}, u32[]{:S(2)}) copy-start(bf16[2,2,512,256]{3,2,1,0:T(8,128)(2,1)S(1)} %get-tuple-element.76) | copy-start | bytes 3145732
  15.3 6.1 %collective-permute-start.1 = (bf16[2,128,512]{2,1,0:T(8,128)(2,1)}, bf16[2,128,512]{2,1,0:T(8,128)(2,1)}, u32[]{:S(2)}, u32[]{:S(2)}) collective-permute-start(bf16[2,128,512]{2,1,0:T(8,128)(2,1)} %collective-permute-done), channel_id=1, source_target_pairs={{0,8},{8,16},{16,24},{24,0},{1,9},{9,17},{17,25},{25,1},{2,10},{10... | collective-permute-start | bytes 786440 | tf_op jit(solution)/shard_map/ppermute | solution.py:14
  57.6 1.0 copy-start.5
  58.5 113.9 %all-reduce.15.cloned.1.call-start = ((), (), s32[]{:S(2)}) async-start(), calls=%async_computation.4 | async-start | bytes 2097152 | tf_op jit(solution)/shard_map/psum | solution.py:29
  60.0 7.2 %copy-start.3 = (bf16[2,512,256]{2,1,0:T(8,128)(2,1)S(1)}, bf16[2,512,256]{2,1,0:T(8,128)(2,1)}, u32[]{:S(2)}) copy-start(bf16[2,512,256]{2,1,0:T(8,128)(2,1)} %slice_bitcast_fusion.6) | copy-start | bytes 1572868
  69.6 190.0 %all-reduce.9.cloned.1.call-start = ((), (), s32[]{:S(2)}) async-start(), calls=%async_computation.1 | async-start | bytes 2097152 | tf_op jit(solution)/shard_map/psum | solution.py:29
  172.4 2.6 copy-start.9
  174.9 1.7 copy-start.2
  174.9 1.7 copy-start.10
  175.0 1.7 copy-start.11
  176.7 1.6 copy-start
  177.3 1.1 copy-start.6
  180.6 1.2 copy-start.7
  180.6 117.0 %all-reduce.13.cloned.1.call-start = ((), (), s32[]{:S(2)}) async-start(), calls=%async_computation.3 | async-start | bytes 2097152 | tf_op jit(solution)/shard_map/psum | solution.py:29
  259.6 38.0 %copy-start.4 = (bf16[2,512,256]{1,2,0:T(8,128)(2,1)S(1)}, bf16[2,512,256]{1,2,0:T(8,128)(2,1)}, u32[]{:S(2)}) copy-start(bf16[2,512,256]{1,2,0:T(8,128)(2,1)} %get-tuple-element.65) | copy-start | bytes 1572868
  299.1 2.0 copy-start.8
  299.1 2.0 copy-start.12
Sparse Core Ops, SparseCore 0:
  9.5 42.8 all-gather.1
  58.6 75.6 all-reduce.10
  136.8 35.4 all-reduce.14
  180.7 78.8 all-reduce.8
  262.1 35.4 all-reduce.12
